TPU v7x, 128 devices: a whole 4x4x4 slice. The times are simulated.
128 devices in a mesh: shard: 8 (over x, core), owner: 16 (over z, y).
Axes of the slice: x: 4, y: 4, z: 4, core: 2. Of those that a mesh axis runs over, the one named last changes fastest.
Arguments:
- gradient: float32 [128, 2048, 768], P('owner', 'shard'), may hold values from -6 to 6
- old_basis: float32 [128, 2048, 256], P('owner', 'shard'), may hold values from -0.125 to 0.125
- moment_one: float32 [128, 256, 768], P('owner', 'shard'), may hold values from -6 to 6
- moment_two: float32 [128, 256, 768], P('owner', 'shard'), may hold values from 0.01 to 1
- slot_expert: int32 [128], replicated, may hold values from 0 to 127, as said below
- cost: int32 [128], replicated, may hold values from 0 to 5
Outputs:
- new_basis: float32 [128, 2048, 256], P('owner', 'shard')
- new_moment_one: float32 [128, 256, 768], P('owner', 'shard')
- new_moment_two: float32 [128, 256, 768], P('owner', 'shard')
- update: bfloat16 [128, 2048, 768], P('owner', 'shard')
Inputs may be any that keep to these rules, and one draw needn't show every extreme that they name: `slot_expert`: A permutation of the 128 experts. Expert e's gradient lies in owner group e // 8; state slot s lies in owner group s // 8. The 8 slots of one owner group hold experts of 8 different owner groups, and the 8 experts of one owner group are held by 8 different owner groups.
All inputs are finite; a program needn't handle non-finite values.
Results may differ from a plain program's by a relative error of at most 0.001.
Values sent between devices are 32-bit elements; how exact they have to be, the bound alone decides.
A program may use at most 192 MiB of HBM per device.

v0:
```python
import jax
import jax.numpy as jnp
from jax import lax
from jax.sharding import PartitionSpec as P

HIGHEST_PREC = lax.Precision.HIGHEST
BETA_ONE = 0.9
BETA_TWO = 0.99
EPSILON = 1e-08
GALORE_SCALE = 0.25


def whole_step(basis_now, grad_now):
    inner_prod = jnp.dot(grad_now.T, basis_now, precision=HIGHEST_PREC)
    tall_block = jnp.dot(grad_now, inner_prod, precision=HIGHEST_PREC)
    gram_matrix = jnp.dot(tall_block.T, tall_block, precision=HIGHEST_PREC)
    factor = jnp.linalg.cholesky(gram_matrix)
    return lax.linalg.triangular_solve(
        factor, tall_block, left_side=False, lower=True, transpose_a=True
    )


def refresh_project(grad_slices, basis_slices, counts):
    slots = grad_slices.shape[0]
    grad_whole, basis_whole = (
        lax.all_to_all(grad_slices, "shard", split_axis=0, concat_axis=1, tiled=True),
        lax.all_to_all(basis_slices, "shard", split_axis=0, concat_axis=1, tiled=True),
    )
    shard_now = lax.axis_index("shard")
    my_count = jnp.sum(jnp.where(jnp.arange(slots) == shard_now, counts, 0))
    grad_now = grad_whole[0]
    basis_new = lax.fori_loop(
        0, my_count, lambda step_index, current: whole_step(current, grad_now), basis_whole[0]
    )
    projected = jnp.dot(basis_new.T, grad_now, precision=HIGHEST_PREC)
    basis_back, proj_back = (
        lax.all_to_all(basis_new[None], "shard", split_axis=1, concat_axis=0, tiled=True),
        lax.all_to_all(projected[None], "shard", split_axis=1, concat_axis=0, tiled=True),
    )
    return (basis_back, proj_back)


def on_device(gradient, old_basis, moment_one, moment_two, slot_expert, cost):
    slots = gradient.shape[0]
    owners = lax.axis_size("owner")
    owner_now = lax.axis_index("owner")
    table = slot_expert.reshape(owners, slots)
    mine = lax.dynamic_index_in_dim(table, owner_now, 0, keepdims=False)
    home_pick = (mine[:, None] // slots == jnp.arange(owners)[None, :]).astype(jnp.float32)
    own_ids = owner_now * slots + jnp.arange(slots)
    send_pick = jnp.sum((table[:, :, None] == own_ids[None, None, :]).astype(jnp.float32), axis=1)
    slot_counts = jnp.sum(
        jnp.where(mine[:, None] == jnp.arange(cost.shape[0])[None, :], cost[None, :], 0), axis=1
    )
    outgoing = jnp.einsum("oi,irc->orc", send_pick, gradient, precision=HIGHEST_PREC)
    arrived = lax.all_to_all(outgoing, "owner", split_axis=0, concat_axis=0, tiled=True)
    slot_grad = jnp.einsum("jh,hrc->jrc", home_pick, arrived, precision=HIGHEST_PREC)
    basis_slot, projected = refresh_project(slot_grad, old_basis, slot_counts)
    moment_new = BETA_ONE * moment_one + (1.0 - BETA_ONE) * projected
    second_new = BETA_TWO * moment_two + (1.0 - BETA_TWO) * projected * projected
    normed = moment_new / (jnp.sqrt(second_new) + EPSILON)
    expanded = jnp.einsum(
        "krq,kqc->krc",
        basis_slot,
        lax.all_gather(normed, "shard", axis=1, tiled=True),
        precision=HIGHEST_PREC,
    )
    update = (GALORE_SCALE * expanded).astype(jnp.bfloat16)
    return (basis_slot, moment_new, second_new, update)


def solution(mesh):
    in_specs = (
        P("owner", "shard", None),
        P("owner", "shard", None),
        P("owner", "shard", None),
        P("owner", "shard", None),
        P(),
        P(),
    )
    out_specs = (
        P("owner", "shard", None),
        P("owner", "shard", None),
        P("owner", "shard", None),
        P("owner", "shard", None),
    )
    return jax.shard_map(
        on_device, mesh=mesh, in_specs=in_specs, out_specs=out_specs, check_vma=False
    )
```

profile of v0, /device:TPU:1, one launch (start us, length us, event | category | flops | bytes accessed | tf_op | source)
XLA Modules:
  0.0 882.7 jit_solution(13709281338159190592)
XLA Ops:
  7.2 0.7 reshape.109
  7.9 0.1 copy.29
  8.0 0.1 convert_reduce_fusion
  8.1 17.5 %fusion.10 = f32[16,256,768]{2,0,1:T(8,128)} fusion(f32[8,256,768]{2,1,0:T(8,128)} %param.8, f32[16,8]{0,1:T(8,128)S(1)} %convert_reduce_fusion), kind=kOutput, calls=%fused_computation.30 | convolution fusion | flops 301989888 | bytes 18874880 | tf_op jit(solution)/shard_map/oi,irc->orc/dot_general | solution.py:55
  25.6 16.4 %copy.31 = f32[16,256,768]{2,1,0:T(8,128)} copy(f32[16,256,768]{2,0,1:T(8,128)} %fusion.10) | data formatting | bytes 25165824 | tf_op jit(solution)/shard_map/oi,irc->orc/dot_general | solution.py:55
  42.0 148.4 %all_to_all.47 = f32[16,256,768]{2,1,0:T(8,128)} all-to-all(f32[16,256,768]{2,1,0:T(8,128)} %copy.31), channel_id=1, replica_groups=mesh['shard'=8,'owner'=16] {'owner'}, dimensions={0} | all-to-all | bytes 25165824 | tf_op jit(solution)/shard_map/all_to_all | solution.py:56
  190.4 6.8 all-to-all-start
  197.2 16.5 %fusion.8 = f32[8,256,768]{2,0,1:T(8,128)S(1)} fusion(f32[16,256,768]{2,1,0:T(8,128)} %all_to_all.47, s32[8]{0:T(128)S(1)} %get-tuple-element.55), kind=kOutput, calls=%fused_computation.28 | convolution fusion | flops 301990016 | bytes 18874400 | tf_op jit(solution)/shard_map/jh,hrc->jrc/dot_general | solution.py:57
  213.8 4.6 copy.33
  218.4 0.0 copy-start.4
  218.4 5.1 all-to-all-done
  223.5 0.0 copy-start
  223.5 1.3 copy-done
  224.8 5.5 all-to-all-start.2
  230.3 0.0 all-gather.2.cloned.1.call-start
  230.3 0.0 copy-done.4
  230.3 0.2 select_reduce_fusion.2
  230.5 0.6 fusion.17
  231.1 1.9 copy.37
  233.1 68.6 %all-to-all-done.2 = f32[8,256,768]{2,1,0:T(8,128)} async-done(((f32[8,256,768]{2,1,0:T(8,128)}), f32[8,256,768]{2,1,0:T(8,128)}, u32[]{:S(2)}, u32[]{:S(2)}) %all-to-all-start.2) | async-done | bytes 6291488 | tf_op jit(solution)/shard_map/all_to_all | solution.py:26
  301.7 0.8 while.13
  302.5 7.6 convolution_bitcast_fusion
  310.1 0.0 copy-start.2
  310.1 0.0 copy-start.3
  310.1 0.8 copy.35
  310.9 491.6 %all_to_all.48 = f32[1,256,768]{2,0,1:T(1,128)S(1)} all-to-all(f32[1,256,768]{2,0,1:T(1,128)S(1)} %copy.35), channel_id=1, replica_groups=mesh['shard'=8,'owner'=16] {'shard'}, dimensions={1} | all-to-all | bytes 1572864 | tf_op jit(solution)/shard_map/all_to_all | solution.py:38
  802.5 0.1 copy.40
  802.6 0.0 copy-done.2
  802.6 0.0 copy-done.3
  802.6 1.6 add_divide_fusion
  804.2 0.0 all-gather.2.cloned.1.call-update
  804.3 3.6 copy.38
  807.9 53.6 %all_to_all.49 = f32[1,2048,256]{2,0,1:T(1,128)S(1)} all-to-all(f32[1,2048,256]{2,0,1:T(1,128)} %copy.38), channel_id=1, replica_groups=mesh['shard'=8,'owner'=16] {'shard'}, dimensions={1} | all-to-all | bytes 4194304 | tf_op jit(solution)/shard_map/all_to_all | solution.py:37
  861.5 0.1 copy.39
  861.6 0.0 copy-start.1
  861.6 2.6 all-gather.2.cloned.1.call-done
  864.2 11.6 %multiply_convert_fusion = bf16[8,256,768]{2,1,0:T(8,128)(2,1)} fusion(f32[8,256,256]{2,1,0:T(8,128)S(1)} %bitcast.92, f32[8,256,768]{2,1,0:T(8,128)} %all-gather.2.cloned.1.call-done), kind=kOutput, calls=%fused_computation.32 | convolution fusion | flops 4834983936 | bytes 11534336 | tf_op jit(solution)/shard_map/krq,kqc->krc/dot_general | solution.py:62
  875.8 0.0 copy-done.1
  (2 shorter events, 0.0 us)
Async XLA Ops:
  190.4 33.1 %all-to-all-start = ((f32[8,256,256]{2,1,0:T(8,128)}), f32[8,256,256]{2,1,0:T(8,128)S(1)}, u32[]{:S(2)}, u32[]{:S(2)}) async-start(f32[8,256,256]{2,1,0:T(8,128)} %param.9), calls=%async_computation | async-start | bytes 4194304 | tf_op jit(solution)/shard_map/all_to_all | solution.py:27
  218.4 11.9 %copy-start.4 = (s32[128]{0:T(128)S(1)}, s32[128]{0:T(128)}, u32[]{:S(2)}) copy-start(s32[128]{0:T(128)} %param.13) | copy-start | bytes 1540
  223.5 1.3 copy-start
  224.8 76.9 %all-to-all-start.2 = ((f32[8,256,768]{2,1,0:T(8,128)}), f32[8,256,768]{2,1,0:T(8,128)}, u32[]{:S(2)}, u32[]{:S(2)}) async-start(f32[8,256,768]{2,1,0:T(8,128)} %copy.33), calls=%async_computation.2 | async-start | bytes 12582912 | tf_op jit(solution)/shard_map/all_to_all | solution.py:26
  230.3 633.9 %all-gather.2.cloned.1.call-start = ((), (), s32[]{:S(2)}) async-start(), calls=%async_computation.5 | async-start | bytes 7077888 | tf_op jit(solution)/shard_map/all_gather | solution.py:65
  310.1 492.5 %copy-start.2 = (f32[8,32,768]{2,1,0:T(8,128)S(1)}, f32[8,32,768]{2,1,0:T(8,128)}, u32[]{:S(2)}) copy-start(f32[8,32,768]{2,1,0:T(8,128)} %param.11) | copy-start | bytes 2359300
  310.1 492.5 %copy-start.3 = (f32[8,32,768]{2,1,0:T(8,128)S(1)}, f32[8,32,768]{2,1,0:T(8,128)}, u32[]{:S(2)}) copy-start(f32[8,32,768]{2,1,0:T(8,128)} %param.10) | copy-start | bytes 2359300
  861.6 14.2 %copy-start.1 = (f32[1,2048,256]{2,1,0:T(8,128)}, f32[1,2048,256]{2,1,0:T(8,128)S(1)}, u32[]{:S(2)}) copy-start(f32[1,2048,256]{2,1,0:T(8,128)S(1)} %copy.39) | copy-start | bytes 6291460
Sparse Core Ops, SparseCore 0:
  804.4 59.7 all-gather.1
where the time goes:
time: 888 us; the launch traced here: 883 us
  blocking collectives  694 us (78%)
  waiting for transfers between devices  76.4 us (9%)
  matrix products  53.2 us (6%)
  local copies, waits for them, and re-layouts  29.7 us (3%)
  between operations  14.2 us (2%)
  starting transfers between devices  12.3 us (1%)
    all_to_all x1, blocking collectives, refresh_project(): lax.all_to_all(projected[None], 'shard', split_axis=1, concat_axis=0, til...  492 us
    all_to_all x1, blocking collectives, on_device(): lax.all_to_all(outgoing, 'owner', split_axis=0, concat_axis=0, tiled=True)  148 us
    all_to_all x1, waiting for transfers between devices, refresh_project(): lax.all_to_all(grad_slices, 'shard', split_axis=0, concat_axis=1, tiled=T...  68.6 us
    all_to_all x1, blocking collectives, refresh_project(): lax.all_to_all(basis_new[None], 'shard', split_axis=1, concat_axis=0, til...  53.6 us
  transfers between devices with their start and end apart: 3, of which 3 were waited for; matrix products, arithmetic and copies ran while one was open for 3% of the time, Pallas kernels for 0%

commit v1 on v0

--- a/solution.py
+++ b/solution.py
@@ -35,7 +35,12 @@
     projected = jnp.dot(basis_new.T, grad_now, precision=HIGHEST_PREC)
     basis_back, proj_back = (
         lax.all_to_all(basis_new[None], "shard", split_axis=1, concat_axis=0, tiled=True),
-        lax.all_to_all(projected[None], "shard", split_axis=1, concat_axis=0, tiled=True),
+        jnp.concatenate(
+            lax.all_to_all(
+                jnp.stack(jnp.split(projected[None], lax.axis_size("shard"), axis=1)), "shard", 0, 0
+            ),
+            axis=0,
+        ),
     )
     return (basis_back, proj_back)
 

time: 888 us -> 880 us (level)
  no operation moved by 1% of the time
where the time goes in v1:
time: 880 us; the launch traced here: 876 us
  blocking collectives  687 us (78%)
  waiting for transfers between devices  76.4 us (9%)
  matrix products  53.2 us (6%)
  local copies, waits for them, and re-layouts  28.9 us (3%)
  between operations  14.2 us (2%)
  starting transfers between devices  12.3 us (1%)
    all_to_all x1, blocking collectives, refresh_project(): lax.all_to_all(jnp.stack(jnp.split(projected[None], lax.axis_size('shard'...  485 us
    all_to_all x1, blocking collectives, on_device(): lax.all_to_all(outgoing, 'owner', split_axis=0, concat_axis=0, tiled=True)  148 us
    all_to_all x1, waiting for transfers between devices, refresh_project(): lax.all_to_all(grad_slices, 'shard', split_axis=0, concat_axis=1, tiled=T...  68.6 us
    all_to_all x1, blocking collectives, refresh_project(): lax.all_to_all(basis_new[None], 'shard', split_axis=1, concat_axis=0, til...  53.6 us
  transfers between devices with their start and end apart: 3, of which 3 were waited for; matrix products, arithmetic and copies ran while one was open for 3% of the time, Pallas kernels for 0%

profile of v1, /device:TPU:1, one launch (start us, length us, event | category | flops | bytes accessed | tf_op | source)
XLA Modules:
  0.0 875.6 jit_solution(7950947707604090853)
XLA Ops:
  7.2 0.7 reshape.109
  7.9 0.1 copy.28
  8.0 0.1 convert_reduce_fusion
  8.1 17.5 %fusion.10 = f32[16,256,768]{2,0,1:T(8,128)} fusion(f32[8,256,768]{2,1,0:T(8,128)} %param.8, f32[16,8]{0,1:T(8,128)S(1)} %convert_reduce_fusion), kind=kOutput, calls=%fused_computation.30 | convolution fusion | flops 301989888 | bytes 18874880 | tf_op jit(solution)/shard_map/oi,irc->orc/dot_general | solution.py:60
  25.6 16.4 %copy.30 = f32[16,256,768]{2,1,0:T(8,128)} copy(f32[16,256,768]{2,0,1:T(8,128)} %fusion.10) | data formatting | bytes 25165824 | tf_op jit(solution)/shard_map/oi,irc->orc/dot_general | solution.py:60
  42.0 148.4 %all_to_all.40 = f32[16,256,768]{2,1,0:T(8,128)} all-to-all(f32[16,256,768]{2,1,0:T(8,128)} %copy.30), channel_id=1, replica_groups=mesh['shard'=8,'owner'=16] {'owner'}, dimensions={0} | all-to-all | bytes 25165824 | tf_op jit(solution)/shard_map/all_to_all | solution.py:61
  190.4 6.8 all-to-all-start
  197.2 16.5 %fusion.8 = f32[8,256,768]{2,0,1:T(8,128)S(1)} fusion(f32[16,256,768]{2,1,0:T(8,128)} %all_to_all.40, s32[8]{0:T(128)S(1)} %get-tuple-element.55), kind=kOutput, calls=%fused_computation.28 | convolution fusion | flops 301990016 | bytes 18874400 | tf_op jit(solution)/shard_map/jh,hrc->jrc/dot_general | solution.py:62
  213.8 4.6 copy.32
  218.4 0.0 copy-start.4
  218.4 5.0 all-to-all-done
  223.4 0.0 copy-start
  223.4 1.3 copy-done
  224.7 5.5 all-to-all-start.2
  230.2 0.0 all-gather.2.cloned.1.call-start
  230.2 0.0 copy-done.4
  230.2 0.2 select_reduce_fusion.2
  230.4 0.6 fusion.26
  231.0 1.9 copy.35
  232.9 68.6 %all-to-all-done.2 = f32[8,256,768]{2,1,0:T(8,128)} async-done(((f32[8,256,768]{2,1,0:T(8,128)}), f32[8,256,768]{2,1,0:T(8,128)}, u32[]{:S(2)}, u32[]{:S(2)}) %all-to-all-start.2) | async-done | bytes 6291488 | tf_op jit(solution)/shard_map/all_to_all | solution.py:26
  301.6 0.8 while.13
  302.4 7.6 convolution_bitcast_fusion
  310.0 0.0 copy-start.2
  310.0 0.0 copy-start.3
  310.1 485.3 %all_to_all.41 = f32[8,1,32,768]{3,2,1,0:T(8,128)S(1)} all-to-all(f32[8,1,32,768]{3,2,1,0:T(8,128)S(1)} %fusion.14), channel_id=1, replica_groups=mesh['shard'=8,'owner'=16] {'shard'}, dimensions={0} | all-to-all | bytes 1572864 | tf_op jit(solution)/shard_map/all_to_all | solution.py:39
  795.5 0.0 copy-done.2
  795.5 0.0 copy-done.3
  795.5 1.6 add_divide_fusion
  797.1 0.0 all-gather.2.cloned.1.call-update
  797.1 3.6 copy.36
  800.7 53.6 %all_to_all.42 = f32[1,2048,256]{2,0,1:T(1,128)S(1)} all-to-all(f32[1,2048,256]{2,0,1:T(1,128)} %copy.36), channel_id=1, replica_groups=mesh['shard'=8,'owner'=16] {'shard'}, dimensions={1} | all-to-all | bytes 4194304 | tf_op jit(solution)/shard_map/all_to_all | solution.py:37
  854.3 0.1 copy.37
  854.4 0.0 copy-start.1
  854.4 2.7 all-gather.2.cloned.1.call-done
  857.2 11.6 %multiply_convert_fusion = bf16[8,256,768]{2,1,0:T(8,128)(2,1)} fusion(f32[8,256,256]{2,1,0:T(8,128)S(1)} %bitcast.130, f32[8,256,768]{2,1,0:T(8,128)} %all-gather.2.cloned.1.call-done), kind=kOutput, calls=%fused_computation.32 | convolution fusion | flops 4834983936 | bytes 11534336 | tf_op jit(solution)/shard_map/krq,kqc->krc/dot_general | solution.py:67
  868.8 0.0 copy-done.1
  (10 shorter events, 0.1 us)
Async XLA Ops:
  190.4 33.0 %all-to-all-start = ((f32[8,256,256]{2,1,0:T(8,128)}), f32[8,256,256]{2,1,0:T(8,128)S(1)}, u32[]{:S(2)}, u32[]{:S(2)}) async-start(f32[8,256,256]{2,1,0:T(8,128)} %param.9), calls=%async_computation | async-start | bytes 4194304 | tf_op jit(solution)/shard_map/all_to_all | solution.py:27
  218.4 11.8 %copy-start.4 = (s32[128]{0:T(128)S(1)}, s32[128]{0:T(128)}, u32[]{:S(2)}) copy-start(s32[128]{0:T(128)} %param.13) | copy-start | bytes 1540
  223.4 1.3 copy-start
  224.7 76.9 %all-to-all-start.2 = ((f32[8,256,768]{2,1,0:T(8,128)}), f32[8,256,768]{2,1,0:T(8,128)}, u32[]{:S(2)}, u32[]{:S(2)}) async-start(f32[8,256,768]{2,1,0:T(8,128)} %copy.32), calls=%async_computation.2 | async-start | bytes 12582912 | tf_op jit(solution)/shard_map/all_to_all | solution.py:26
  230.2 627.0 %all-gather.2.cloned.1.call-start = ((), (), s32[]{:S(2)}) async-start(), calls=%async_computation.5 | async-start | bytes 7077888 | tf_op jit(solution)/shard_map/all_gather | solution.py:70
  310.0 485.5 %copy-start.2 = (f32[8,32,768]{2,1,0:T(8,128)S(1)}, f32[8,32,768]{2,1,0:T(8,128)}, u32[]{:S(2)}) copy-start(f32[8,32,768]{2,1,0:T(8,128)} %param.11) | copy-start | bytes 2359300
  310.0 485.5 %copy-start.3 = (f32[8,32,768]{2,1,0:T(8,128)S(1)}, f32[8,32,768]{2,1,0:T(8,128)}, u32[]{:S(2)}) copy-start(f32[8,32,768]{2,1,0:T(8,128)} %param.10) | copy-start | bytes 2359300
  854.4 14.4 %copy-start.1 = (f32[1,2048,256]{2,1,0:T(8,128)}, f32[1,2048,256]{2,1,0:T(8,128)S(1)}, u32[]{:S(2)}) copy-start(f32[1,2048,256]{2,1,0:T(8,128)S(1)} %copy.37) | copy-start | bytes 6291460
Sparse Core Ops, SparseCore 0:
  797.2 59.8 all-gather.1
